TPU v7x, 256 devices: a whole 4x4x8 slice. The times are simulated.
256 devices in a mesh: req: 32 (over y, z), head: 2 (over core), grp: 4 (over x).
Axes of the slice: x: 4, y: 4, z: 8, core: 2. Of those that a mesh axis runs over, the one named last changes fastest.
Arguments:
- residual: bfloat16 [1024, 7168], P(('req', 'grp'), 'head'), may hold values from -12 to 12
- attn_part: bfloat16 [2, 1024, 7168], P('head', ('req', 'grp')), may hold values from -6 to 6
- norm_gain: float32 [7168], P('head'), may hold values from 0.1 to 1.9
- routes: int32 [1024, 8], P(('req', 'grp')), may hold values from 0 to 31, all different within a row; in each aligned block of 8 rows (0 to 7, 8 to 15, ...) at most 4 rows name the same one
- gates: float32 [1024, 8], P(('req', 'grp')), may hold values from 0.1 to 0.6
- gate_weight: bfloat16 [32, 7168, 2048], P('req', None, ('head', 'grp')), may hold values from -0.0625 to 0.0625
- up_weight: bfloat16 [32, 7168, 2048], P('req', None, ('head', 'grp')), may hold values from -0.0625 to 0.0625
- down_weight: bfloat16 [32, 2048, 7168], P('req', None, ('head', 'grp')), may hold values from -0.125 to 0.125
Outputs:
- mixed: bfloat16 [1024, 7168], P(('req', 'grp'), 'head')
Inputs may be any that keep to these rules, and one draw needn't show every extreme that they name: `routes`: each row names 8 different experts. In each aligned block of 8 rows (the rows of one index pair of req and grp) no expert is named more than 4 times, a bound that some block reaches.
All inputs are finite; a program needn't handle non-finite values.
Results may differ from a plain program's by a relative error of at most 0.012.
Values may be sent and summed in bfloat16 or wider, within the bound.
A program may use at most 128 MiB of HBM per device.

v0:
```python
import jax
import jax.numpy as jnp
from jax import lax
from jax.sharding import PartitionSpec as P

D = 7168
CAP = 4


EPSILON = 1e-06


def slot_places(routes, experts):
    count_rows, count_top = routes.shape
    flat_routes = routes.reshape(count_rows * count_top)
    onehot = (flat_routes[:, None] == jnp.arange(experts, dtype=jnp.int32)[None, :]).astype(
        jnp.int32
    )
    earlier = jnp.cumsum(onehot, axis=0) - onehot
    slot_index = jnp.sum(earlier * onehot, axis=1).reshape(count_rows, count_top)
    return routes * CAP + slot_index


def select_table(places, experts):
    return places[:, :, None] == jnp.arange(experts * CAP, dtype=jnp.int32)[None, None, :]


def expert_hidden(arrived, gate_weight, up_weight):
    groups, sources, columns, features = arrived.shape
    local_experts = gate_weight.shape[0]
    shaped = arrived.reshape(groups, sources, local_experts, columns // local_experts, features)
    gate_act = jnp.einsum(
        "gresd,edf->gresf", shaped, gate_weight, preferred_element_type=jnp.float32
    )
    up_act = jnp.einsum("gresd,edf->gresf", shaped, up_weight, preferred_element_type=jnp.float32)
    return (jax.nn.silu(gate_act) * up_act).astype(jnp.bfloat16)


def on_device(residual, attn_part, norm_gain, routes, gates, gate_weight, up_weight, down_weight):
    req_count = lax.axis_size("req")
    experts = gate_weight.shape[0] * req_count
    summed = lax.psum_scatter(
        attn_part[0].astype(jnp.float32).astype(jnp.bfloat16),
        "head",
        scatter_dimension=1,
        tiled=True,
    ).astype(jnp.float32)
    hidden_state = residual.astype(jnp.float32) + summed
    squares = lax.psum(jnp.sum(hidden_state * hidden_state, axis=1), "head")
    row_scale = lax.rsqrt(squares / D + EPSILON)
    normed = (hidden_state * row_scale[:, None] * norm_gain[None, :]).astype(jnp.bfloat16)
    selected = select_table(slot_places(routes, experts), experts)
    weighting = jnp.sum(jnp.where(selected, gates[:, :, None], 0.0), axis=1)
    packing = jnp.any(selected, axis=1).astype(jnp.bfloat16)
    packed = jnp.einsum("tj,td->jd", packing, normed, preferred_element_type=jnp.float32).astype(
        jnp.bfloat16
    )
    packed = packed.reshape(req_count, -1, normed.shape[1])
    arrived = lax.all_to_all(packed, "req", split_axis=0, concat_axis=0, tiled=True)
    whole_rows = lax.all_gather(arrived, "head", axis=2, tiled=True)
    hidden_units = expert_hidden(
        lax.all_gather(whole_rows[None], "grp", axis=0, tiled=True), gate_weight, up_weight
    )
    projected = jnp.einsum(
        "gresf,efd->gresd",
        lax.all_gather(hidden_units, ("head", "grp"), axis=4, tiled=True),
        down_weight,
        preferred_element_type=jnp.float32,
    )
    outgoing = projected.astype(jnp.bfloat16)
    regrouped = lax.all_to_all(outgoing, "grp", split_axis=0, concat_axis=4, tiled=True)
    regrouped = regrouped.reshape(req_count, -1, regrouped.shape[4])
    returned = lax.all_to_all(regrouped, "req", split_axis=0, concat_axis=0, tiled=True)
    back_rows = returned.reshape(-1, returned.shape[-1]).astype(jnp.float32)
    routed = jnp.dot(weighting, back_rows, precision=lax.Precision.HIGHEST)
    return (hidden_state + routed).astype(jnp.bfloat16)


def solution(mesh):
    placed = (
        P(("req", "grp"), "head"),
        P("head", ("req", "grp"), None),
        P("head"),
        P(("req", "grp"), None),
        P(("req", "grp"), None),
        P("req", None, ("head", "grp")),
        P("req", None, ("head", "grp")),
        P("req", None, ("head", "grp")),
    )
    return jax.shard_map(
        on_device, mesh=mesh, in_specs=placed, out_specs=P(("req", "grp"), "head"), check_vma=False
    )
```

profile of v0, /device:TPU:32, one launch (start us, length us, event | category | flops | bytes accessed | tf_op | source)
XLA Modules:
  0.0 268.5 jit_solution(15193154326299129199)
XLA Ops:
  6.5 0.0 reduce-scatter.2.cloned.1.call-start
  6.5 0.7 reduce-scatter.2.cloned.1.call-update
  7.3 0.0 all-gather.5.cloned.1.call-start
  7.3 0.8 eq.28
  8.1 0.1 fusion.43
  8.1 0.1 reduce_window_sum.11
  8.2 0.2 select_reduce_fusion.1
  8.4 0.1 reshape.39
  8.5 0.7 multiply_add_fusion
  9.2 16.0 %reduce-scatter.2.cloned.1.call-done = bf16[8,3584]{1,0:T(8,128)(2,1)} async-done(((bf16[8,7168]{1,0:T(8,128)(2,1)}), bf16[8,3584]{1,0:T(8,128)(2,1)}) %reduce-scatter.2.cloned.1.call-update) | async-done | bytes 57360 | tf_op jit(solution)/shard_map/reduce_scatter | solution.py:42
  25.3 1.0 multiply_reduce_fusion
  26.3 0.1 fusion.42
  26.3 2.5 psum.7
  28.8 1.3 convolution_convert_fusion
  30.1 0.2 reshape.40
  30.4 36.0 %all_to_all.25 = bf16[32,4,3584]{2,1,0:T(4,128)(2,1)S(1)} all-to-all(bf16[32,4,3584]{2,1,0:T(4,128)(2,1)S(1)} %reshape.40), channel_id=1, replica_groups=mesh['req'=32,'head'=2,'grp'=4] {'req'}, dimensions={0} | all-to-all | bytes 1835008 | tf_op jit(solution)/shard_map/all_to_all | solution.py:59
  66.3 1.1 copy.24
  67.4 0.0 all-gather.5.cloned.1.call-update
  67.4 0.0 all-gather.9.cloned.1.call-start
  67.5 12.1 %all-gather.5.cloned.1.call-done = bf16[32,4,7168]{2,0,1:T(8,128)(2,1)} async-done(((bf16[32,4,3584]{2,0,1:T(8,128)(2,1)}), bf16[32,4,7168]{2,0,1:T(8,128)(2,1)}) %all-gather.5.cloned.1.call-update) | async-done | bytes 1835024 | tf_op jit(solution)/shard_map/all_gather | solution.py:60
  79.6 0.0 all-gather.9.cloned.1.call-update
  79.6 0.0 all-gather.7.cloned.1.call-start
  79.7 80.0 %all-gather.9.cloned.1.call-done = bf16[128,4,7168]{2,0,1:T(8,128)(2,1)} async-done(((bf16[32,4,7168]{2,0,1:T(8,128)(2,1)}), bf16[128,4,7168]{2,0,1:T(8,128)(2,1)}) %all-gather.9.cloned.1.call-update) | async-done | bytes 7340048 | tf_op jit(solution)/shard_map/all_gather | solution.py:62
  159.7 0.0 copy-start.3
  159.7 0.0 copy-start.4
  159.7 6.3 %fusion.20 = f32[4,32,1,4,256]{4,1,3,0,2:T(8,128)S(1)} fusion(bf16[1,7168,256]{2,1,0:T(8,128)(2,1)} %param.13, bf16[4,32,4,7168]{3,1,0,2:T(8,128)(2,1)} %bitcast.76), kind=kOutput, calls=%fused_computation.14 | convolution fusion | flops 1879048192 | bytes 11534336 | tf_op jit(solution)/shard_map/gresd,edf->gresf/dot_general | solution.py:32
  166.0 0.0 copy-done.3
  166.0 0.9 copy-done.4
  166.9 2.8 %fusion.35 = bf16[4,32,1,4,256]{4,1,3,0,2:T(8,128)(2,1)} fusion(bf16[1,7168,256]{2,1,0:T(8,128)(2,1)S(1)} %copy-done.4, bf16[4,32,4,7168]{3,1,0,2:T(8,128)(2,1)S(1)} %bitcast.77, f32[4,32,1,4,256]{4,1,3,0,2:T(8,128)S(1)} %fusion.20), kind=kOutput, calls=%fused_computation.17 | convolution fusion | flops 1879834624 | bytes 11796480 | tf_op jit(solution)/shard_map/gresd,edf->gresf/dot_general | solution.py:35
  169.7 0.0 all-gather.7.cloned.1.call-update
  169.7 30.8 %all-gather.7.cloned.1.call-done = bf16[4,32,1,4,2048]{4,1,3,0,2:T(8,128)(2,1)} async-done(((bf16[4,32,1,4,256]{4,1,3,0,2:T(8,128)(2,1)}), bf16[4,32,1,4,2048]{4,1,3,0,2:T(8,128)(2,1)}) %all-gather.7.cloned.1.call-update) | async-done | bytes 2097168 | tf_op jit(solution)/shard_map/all_gather | solution.py:66
  200.5 5.0 %fusion.15 = bf16[4,32,1,4,896]{4,1,3,2,0:T(8,128)(2,1)S(1)} fusion(bf16[1,2048,896]{2,1,0:T(8,128)(2,1)} %param.15, bf16[4,32,1,4,2048]{4,1,3,0,2:T(8,128)(2,1)} %all-gather.7.cloned.1.call-done), kind=kOutput, calls=%fused_computation.13 | convolution fusion | flops 1879506944 | bytes 6684672 | tf_op jit(solution)/shard_map/gresf,efd->gresd/dot_general | solution.py:64
  205.5 0.0 copy-start.2
  205.6 17.9 %all_to_all.26 = bf16[4,32,1,4,896]{4,1,3,2,0:T(8,128)(2,1)S(1)} all-to-all(bf16[4,32,1,4,896]{4,1,3,2,0:T(8,128)(2,1)S(1)} %fusion.15), channel_id=1, replica_groups=mesh['req'=32,'head'=2,'grp'=4] {'grp'}, dimensions={0} | all-to-all | bytes 1835008 | tf_op jit(solution)/shard_map/all_to_all | solution.py:71
  223.4 0.0 copy-start
  223.4 0.0 copy-start.1
  223.4 0.7 copy.33
  224.2 1.3 reshape.51
  225.4 10.1 %all-to-all-start.2 = ((bf16[32,4,3584]{2,1,0:T(4,128)(2,1)}), bf16[32,4,3584]{2,1,0:T(4,128)(2,1)S(1)}, u32[]{:S(2)}, u32[]{:S(2)}) async-start(bf16[32,4,3584]{2,1,0:T(4,128)(2,1)} %reshape.51), calls=%async_computation.3 | async-start | bytes 1835008 | tf_op jit(solution)/shard_map/all_to_all | solution.py:73
  235.5 0.0 copy-done.2
  235.5 0.1 select_reduce_fusion
  235.6 25.0 %all-to-all-done.2 = bf16[32,4,3584]{2,1,0:T(4,128)(2,1)S(1)} async-done(((bf16[32,4,3584]{2,1,0:T(4,128)(2,1)}), bf16[32,4,3584]{2,1,0:T(4,128)(2,1)S(1)}, u32[]{:S(2)}, u32[]{:S(2)}) %all-to-all-start.2) | async-done | bytes 917536 | tf_op jit(solution)/shard_map/all_to_all | solution.py:73
  260.6 0.2 reshape.46
  260.9 0.0 copy-done
  260.9 0.0 copy-done.1
  260.9 1.1 fusion.4
  (1 shorter events, 0.0 us)
Async XLA Ops:
  6.5 18.7 %reduce-scatter.2.cloned.1.call-start = ((), (), s32[]{:S(2)}) async-start(), calls=%async_computation.4 | async-start | bytes 172032 | tf_op jit(solution)/shard_map/reduce_scatter | solution.py:42
  7.3 72.4 %all-gather.5.cloned.1.call-start = ((), (), s32[]{:S(2)}) async-start(), calls=%async_computation.5 | async-start | bytes 2752512 | tf_op jit(solution)/shard_map/all_gather | solution.py:60
  67.4 92.2 %all-gather.9.cloned.1.call-start = ((), (), s32[]{:S(2)}) async-start(), calls=%async_computation.7 | async-start | bytes 9175040 | tf_op jit(solution)/shard_map/all_gather | solution.py:62
  79.6 120.9 %all-gather.7.cloned.1.call-start = ((), (), s32[]{:S(2)}) async-start(), calls=%async_computation.6 | async-start | bytes 2359296 | tf_op jit(solution)/shard_map/all_gather | solution.py:66
  159.7 6.3 %copy-start.3 = (bf16[128,4,7168]{2,0,1:T(8,128)(2,1)S(1)}, bf16[128,4,7168]{2,0,1:T(8,128)(2,1)}, u32[]{:S(2)}) copy-start(bf16[128,4,7168]{2,0,1:T(8,128)(2,1)} %all-gather.9.cloned.1.call-done) | copy-start | bytes 22020100
  159.7 7.3 %copy-start.4 = (bf16[1,7168,256]{2,1,0:T(8,128)(2,1)S(1)}, bf16[1,7168,256]{2,1,0:T(8,128)(2,1)}, u32[]{:S(2)}) copy-start(bf16[1,7168,256]{2,1,0:T(8,128)(2,1)} %param.14) | copy-start | bytes 11010052
  205.5 30.0 %copy-start.2 = (f32[8,8]{1,0:T(8,128)S(1)}, f32[8,8]{1,0:T(8,128)}, u32[]{:S(2)}) copy-start(f32[8,8]{1,0:T(8,128)} %param.12) | copy-start | bytes 772
  223.4 37.4 %copy-start = (bf16[8,3584]{1,0:T(8,128)(2,1)S(1)}, bf16[8,3584]{1,0:T(8,128)(2,1)}, u32[]{:S(2)}) copy-start(bf16[8,3584]{1,0:T(8,128)(2,1)} %param.8) | copy-start | bytes 172036
  223.4 37.4 %copy-start.1 = (bf16[8,3584]{1,0:T(8,128)(2,1)S(1)}, bf16[8,3584]{1,0:T(8,128)(2,1)}, u32[]{:S(2)}) copy-start(bf16[8,3584]{1,0:T(8,128)(2,1)} %reduce-scatter.2.cloned.1.call-done) | copy-start | bytes 172036
  225.4 35.2 %all-to-all-start.2 = ((bf16[32,4,3584]{2,1,0:T(4,128)(2,1)}), bf16[32,4,3584]{2,1,0:T(4,128)(2,1)S(1)}, u32[]{:S(2)}, u32[]{:S(2)}) async-start(bf16[32,4,3584]{2,1,0:T(4,128)(2,1)} %reshape.51), calls=%async_computation.3 | async-start | bytes 1835008 | tf_op jit(solution)/shard_map/all_to_all | solution.py:73
Sparse Core Ops, SparseCore 0:
  9.8 15.4 reduce-scatter.1
  67.5 12.0 all-gather.4
  81.4 78.1 all-gather.8
  169.8 30.6 all-gather.6
where the time goes:
time: 269 us
  waiting for transfers between devices  165 us (61%)
  blocking collectives  56.3 us (21%)
  matrix products  16.5 us (6%)
  between operations  13.2 us (5%)
  starting transfers between devices  10.2 us (4%)
  local copies, waits for them, and re-layouts  5.25 us (2%)
    all_gather x1, waiting for transfers between devices, on_device(): lax.all_gather(whole_rows[None], 'grp', axis=0, tiled=True)  80 us
    all_to_all x1, blocking collectives, on_device(): lax.all_to_all(packed, 'req', split_axis=0, concat_axis=0, tiled=True)  36 us
    all_gather x1, waiting for transfers between devices, on_device(): lax.all_gather(hidden_units, ('head', 'grp'), axis=4, tiled=True)  30.8 us
    all_to_all x1, waiting for transfers between devices, on_device(): lax.all_to_all(regrouped, 'req', split_axis=0, concat_axis=0, tiled=True)  25 us
    all_to_all x1, blocking collectives, on_device(): lax.all_to_all(outgoing, 'grp', split_axis=0, concat_axis=4, tiled=True)  17.9 us
    reduce_scatter x1, waiting for transfers between devices, on_device(): lax.psum_scatter(attn_part[0].astype(jnp.float32).astype(jnp.bfloat16), '...  16 us
    all_gather x1, waiting for transfers between devices, on_device(): whole_rows = lax.all_gather(arrived, 'head', axis=2, tiled=True)  12.1 us
    all_to_all x1, starting transfers between devices, on_device(): lax.all_to_all(regrouped, 'req', split_axis=0, concat_axis=0, tiled=True)  10.1 us
  transfers between devices with their start and end apart: 5, of which 5 were waited for; matrix products, arithmetic and copies ran while one was open for 1% of the time, Pallas kernels for 0%

commit v1 on v0

v1 whole, which is shorter than its diff:
```python
import functools

import jax
import jax.numpy as jnp
from jax import lax
from jax.experimental import pallas as pl
from jax.experimental.pallas import tpu as pltpu
from jax.sharding import PartitionSpec as P

MESH = pl.DeviceIdType.MESH
D = 7168
HALF = D // 2
QUART = HALF // 2
CAP = 4
TOK = 8
NX, NY, NZ = 4, 4, 8
FFS = 256
OUTS = 896
EPSILON = 1e-06

ZREL = (0, 1, 7, 2, 6, 3, 5, 4)
YREL = (0, 1, 3, 2)
ZSLOT = {rel: slot for slot, rel in enumerate(ZREL)}
YSLOT = {rel: slot for slot, rel in enumerate(YREL)}


def kernel(
    res_ref,
    attn_ref,
    gain_ref,
    routes_ref,
    gates_ref,
    wg_hbm,
    wu_hbm,
    wd_hbm,
    out_ref,
    wg,
    wu,
    wd,
    ex,
    hid,
    zb,
    zi,
    xi,
    ysel,
    xb,
    acc,
    hb,
    dacc,
    obs,
    rb,
    fs,
    fb,
    wsem,
    ex_s,
    ex_r,
    zb_s,
    zb_r,
    zi_s,
    zi_r,
    xi_s,
    xi_r,
    y_s,
    y_r,
    xn_s,
    xn_r,
    xf_s,
    xf_r,
    sib_s,
    sib_r,
    h_s,
    h_r,
    hs_s,
    hs_r,
    r_s,
    r_r,
    f_s,
    f_r,
):
    req, h, x = lax.axis_index("req"), lax.axis_index("head"), lax.axis_index("grp")
    y, z = req // NZ, req % NZ

    def dev(dx=0, dy=0, dz=0, sib=False):
        return {
            "req": ((y + dy) % NY) * NZ + (z + dz) % NZ,
            "head": 1 - h if sib else h,
            "grp": (x + dx) % NX,
        }

    sends = []

    def send(src, dst, ssem, rsem, to):
        copy = pltpu.make_async_remote_copy(
            src_ref=src, dst_ref=dst, send_sem=ssem, recv_sem=rsem, device_id=to, device_id_type=MESH
        )
        copy.start()
        sends.append(copy)

    def arrived(dst, ssem, rsem):
        pltpu.make_async_remote_copy(
            src_ref=dst, dst_ref=dst, send_sem=ssem, recv_sem=rsem, device_id=dev(sib=True), device_id_type=MESH
        ).wait_recv()

    loads = [
        pltpu.make_async_copy(src.at[0], dst, wsem.at[i])
        for i, (src, dst) in enumerate(((wg_hbm, wg), (wu_hbm, wu), (wd_hbm, wd)))
    ]
    for load in loads:
        load.start()

    bar = pltpu.get_barrier_semaphore()
    peers = [dev(sib=True)] + [dev(dx=d) for d in range(1, NX)]
    peers += [dev(dy=a, dz=b) for a in range(NY) for b in range(NZ) if a or b]
    for peer in peers:
        pl.semaphore_signal(bar, inc=1, device_id=peer, device_id_type=MESH)

    attn = attn_ref[...].astype(jnp.float32)
    res = res_ref[...].astype(jnp.float32)
    ex[0, :, :HALF] = jnp.concatenate([attn[:, :HALF], attn[:, HALF:]], axis=0).astype(jnp.bfloat16)
    ex[0, :, HALF:] = jnp.concatenate([res[:, :QUART], res[:, QUART:]], axis=0).astype(jnp.bfloat16)

    routes = routes_ref[...]
    gates = gates_ref[...]
    column = lax.broadcasted_iota(jnp.int32, (TOK, 128), 1)
    named = jnp.zeros((TOK, 128), jnp.float32)
    value = jnp.zeros((TOK, 128), jnp.float32)
    for k in range(8):
        hit = (routes[:, k : k + 1] == column // CAP).astype(jnp.float32)
        named = named + hit
        value = value + hit * gates[:, k : k + 1]
    row = lax.broadcasted_iota(jnp.int32, (TOK, 128), 0)
    before = jnp.zeros((TOK, 128), jnp.float32)
    for t in range(TOK - 1):
        before = before + jnp.where(row > t, named[t : t + 1, :], 0.0)
    info = jnp.where(before == (column % CAP).astype(jnp.float32), value, 0.0)
    zi[0] = info
    xi[x] = info

    pl.semaphore_wait(bar, len(peers))
    send(ex.at[0], ex.at[1], ex_s.at[0], ex_r.at[0], dev(sib=True))
    order = [(NZ - ZREL[slot]) % NZ for slot in range(1, NZ)]
    for d in order:
        slot = ZSLOT[(-d) % NZ]
        send(zi.at[0], zi.at[slot], zi_s.at[slot], zi_r.at[slot], dev(dz=d))
    for d in (1, 3, 2):
        send(xi.at[x], xi.at[x], xi_s.at[d], xi_r.at[4 - d], dev(dx=d))

    arrived(ex.at[1], ex_s.at[0], ex_r.at[0])
    theirs = ex[1].astype(jnp.float32)
    t_attn = (theirs[:TOK, :HALF], theirs[TOK:, :HALF])
    m_attn = (attn[:, :HALF], attn[:, HALF:])
    t_res = jnp.concatenate([theirs[:TOK, HALF:], theirs[TOK:, HALF:]], axis=1)
    sums = (m_attn[0] + t_attn[0], m_attn[1] + t_attn[1])
    first = h == 0
    own = res + jnp.where(first, sums[0], sums[1])
    other = t_res + jnp.where(first, sums[1], sums[0])
    squares = jnp.sum(own * own, axis=1, keepdims=True) + jnp.sum(other * other, axis=1, keepdims=True)
    scale = lax.rsqrt(squares / D + EPSILON)
    normed = own * scale * gain_ref[...]
    hid[...] = own
    zb[0] = jnp.concatenate([normed[:, :QUART], normed[:, QUART:]], axis=0).astype(jnp.bfloat16)
    for d in order:
        slot = ZSLOT[(-d) % NZ]
        send(zb.at[0], zb.at[slot], zb_s.at[slot], zb_r.at[slot], dev(dz=d))

    left, right = (x + 3) % NX, (x + 1) % NX

    def x_send(c, yr):
        piece = xb.at[c, h, yr, x]
        send(piece, piece, xn_s.at[c, yr, 0], xn_r.at[c, yr, 0], dev(dx=1))
        send(piece, piece, xn_s.at[c, yr, 1], xn_r.at[c, yr, 1], dev(dx=3))
        send(piece, piece, sib_s.at[c, yr, 0], sib_r.at[c, yr, 0], dev(sib=True))

    def x_forward(c, yr):
        for way, source, to in ((0, left, 1), (1, right, 3)):
            piece = xb.at[c, h, yr, source]
            arrived(piece, xn_s.at[c, yr, way], xn_r.at[c, yr, way])
            part = xb.at[c, h, yr, source, :, pl.ds(way * QUART, QUART)]
            send(part, part, xf_s.at[c, yr, way], xf_r.at[c, yr, way], dev(dx=to))
            send(piece, piece, sib_s.at[c, yr, 1 + way], sib_r.at[c, yr, 1 + way], dev(sib=True))

    def x_far(c, yr):
        far = (x + 2) % NX
        for way in (0, 1):
            part = xb.at[c, h, yr, far, :, pl.ds(way * QUART, QUART)]
            arrived(part, xf_s.at[c, yr, way], xf_r.at[c, yr, way])
        piece = xb.at[c, h, yr, far]
        send(piece, piece, sib_s.at[c, yr, 3], sib_r.at[c, yr, 3], dev(sib=True))

    def sib_wait(c):
        for yr in range(NY):
            for kind, source in enumerate((x, left, right, (x + 2) % NX)):
                piece = xb.at[c, 1 - h, yr, source]
                arrived(piece, sib_s.at[c, yr, kind], sib_r.at[c, yr, kind])

    def y_wait(c, yr):
        piece = xb.at[c, h, yr, x]
        arrived(piece, y_s.at[c, yr], y_r.at[c, yr])

    def select(c):
        for slot in range(4 * c, 4 * c + 4):
            if slot:
                arrived(zi.at[slot], zi_s.at[slot], zi_r.at[slot])
                arrived(zb.at[slot], zb_s.at[slot], zb_r.at[slot])
        tables = [(zi[4 * c + j] != 0.0).astype(jnp.bfloat16) for j in range(4)]
        table = jnp.concatenate([t for j in range(4) for t in (tables[j], tables[j])], axis=0)
        rows16 = lax.broadcasted_iota(jnp.int32, (16, 128), 0) % CAP
        cols16 = lax.broadcasted_iota(jnp.int32, (16, 128), 1)
        pick = jnp.concatenate(
            [
                (cols16 == rows16 + (((y + rel) % NY) * NZ + z) * CAP).astype(jnp.float32)
                for rel in YREL
            ],
            axis=0,
        ).astype(jnp.bfloat16)
        small = lax.dot_general(
            pick, table, (((1,), (1,)), ((), ())), preferred_element_type=jnp.float32
        )
        r = lax.broadcasted_iota(jnp.int32, (64, 64), 0)
        m = lax.broadcasted_iota(jnp.int32, (64, 64), 1)
        blocks = zb[4 * c : 4 * c + 4].reshape(64, QUART)
        for u in (0, 1):
            mask = ((r // 4) % 4 == m // 16) & ((m // 8) % 2 == u)
            onehot = jnp.where(mask, small, 0.0).astype(jnp.bfloat16)
            rows = jnp.dot(onehot, blocks, preferred_element_type=jnp.float32).astype(jnp.bfloat16)
            cols = slice(u * QUART, (u + 1) * QUART)
            xb[c, h, 0, x, :, cols] = rows[:16]
            for yr in range(1, NY):
                ysel[c, yr, :, cols] = rows[16 * yr : 16 * yr + 16]
        for yr in (1, 2, 3):
            back = YSLOT[(-YREL[yr]) % NY]
            send(ysel.at[c, yr], xb.at[c, h, back, x], y_s.at[c, back], y_r.at[c, back], dev(dy=YREL[yr]))
        x_send(c, 0)

    def up(c):
        acc[...] = jnp.zeros_like(acc)

        def step(i, carry):
            part = xb[c, i // 2, :, :, :, pl.ds(pl.multiple_of((i % 2) * QUART, QUART), QUART)]
            rows = part.reshape(256, QUART)
            ks = pl.ds(pl.multiple_of(i * QUART, QUART), QUART)
            acc[:, :FFS] += jnp.dot(rows, wg[ks, :], preferred_element_type=jnp.float32)
            acc[:, FFS:] += jnp.dot(rows, wu[ks, :], preferred_element_type=jnp.float32)
            return carry

        lax.fori_loop(0, 4, step, 0)
        gate = acc[:, :FFS]
        hb[c, h * NX + x] = (gate / (1.0 + jnp.exp(-gate)) * acc[:, FFS:]).astype(jnp.bfloat16)
        mine = hb.at[c, h * NX + x]
        for d in (1, 3, 2):
            send(mine, mine, h_s.at[c, d], h_r.at[c, 4 - d], dev(dx=d))
        send(mine, mine, hs_s.at[c, 0], hs_r.at[c, 0], dev(sib=True))

    def h_forward(c):
        for d in (1, 3, 2):
            block = hb.at[c, h * NX + (x + d) % NX]
            arrived(block, h_s.at[c, d], h_r.at[c, d])
            send(block, block, hs_s.at[c, d], hs_r.at[c, d], dev(sib=True))

    def down(c):
        for d in (0, 1, 3, 2):
            block = hb.at[c, (1 - h) * NX + (x + d) % NX]
            arrived(block, hs_s.at[c, d], hs_r.at[c, d])
        for start, width in ((0, 512), (512, 384)):
            total = jnp.zeros((256, width), jnp.float32)
            for b in range(8):
                total = total + jnp.dot(
                    hb[c, b],
                    wd[b * FFS : (b + 1) * FFS, start : start + width],
                    preferred_element_type=jnp.float32,
                )
            dacc[:, start : start + width] = total
        for yr in range(NY):
            for j in range(4):
                rows = jnp.concatenate(
                    [
                        dacc[yr * 64 + xs * 16 + j * 4 : yr * 64 + xs * 16 + j * 4 + 4, :]
                        for xs in range(NX)
                    ],
                    axis=0,
                ).astype(jnp.bfloat16)
                slot = 4 * c + j
                if yr == 0 and slot == 0:
                    rb[req] = rows
                else:
                    obs[c, yr, j] = rows
                    send(
                        obs.at[c, yr, j],
                        rb.at[req],
                        r_s.at[yr, slot],
                        r_r.at[yr, slot],
                        dev(dy=YREL[yr], dz=ZREL[slot]),
                    )

    select(0)
    y_wait(0, 1)
    x_send(0, 1)
    y_wait(0, 2)
    x_send(0, 2)
    y_wait(0, 3)
    x_send(0, 3)
    x_forward(0, 0)
    select(1)
    x_forward(0, 1)
    y_wait(1, 1)
    x_send(1, 1)
    y_wait(1, 2)
    x_send(1, 2)
    x_forward(0, 2)
    y_wait(1, 3)
    x_send(1, 3)
    x_forward(0, 3)
    for yr in range(NY):
        x_far(0, yr)
    for load in loads:
        load.wait()
    x_forward(1, 0)
    sib_wait(0)
    up(0)
    x_forward(1, 1)
    x_forward(1, 2)
    x_forward(1, 3)
    h_forward(0)
    down(0)
    for yr in range(NY):
        x_far(1, yr)
    sib_wait(1)
    up(1)

    for d in (1, 3, 2):
        arrived(xi.at[(x + d) % NX], xi_s.at[d], xi_r.at[d])
    weights = xi[...].reshape(NX * TOK, 128)
    high = weights.astype(jnp.bfloat16)
    low = (weights - high.astype(jnp.float32)).astype(jnp.bfloat16)
    q = lax.broadcasted_iota(jnp.int32, (128, 512), 0)
    m = lax.broadcasted_iota(jnp.int32, (128, 512), 1)
    spread = (q == (m // 16) * CAP + m % CAP).astype(jnp.bfloat16)
    tr = lax.broadcasted_iota(jnp.int32, (32, 512), 0)
    tc = lax.broadcasted_iota(jnp.int32, (32, 512), 1)
    keep = tr // TOK == (tc // CAP) % NX
    wide = [
        jnp.where(keep, jnp.dot(part, spread, preferred_element_type=jnp.float32), 0.0).astype(jnp.bfloat16)
        for part in (high, low)
    ]

    h_forward(1)
    down(1)
    for yr in range(NY):
        for slot in range(NZ):
            if yr or slot:
                source = ((y - YREL[yr]) % NY) * NZ + (z - ZREL[slot]) % NZ
                arrived(rb.at[source], r_s.at[yr, slot], r_r.at[yr, slot])
    back = rb[...].reshape(512, OUTS)
    mixed = jnp.dot(wide[0], back, preferred_element_type=jnp.float32)
    mixed = mixed + jnp.dot(wide[1], back, preferred_element_type=jnp.float32)
    fs[...] = mixed.reshape(NX, TOK, OUTS)
    fb[x] = fs[x]
    for d in (1, 3, 2):
        send(fs.at[(x + d) % NX], fb.at[x], f_s.at[d], f_r.at[4 - d], dev(dx=d))
    for d in (1, 3, 2):
        arrived(fb.at[(x + d) % NX], f_s.at[d], f_r.at[d])
    for g in range(NX):
        cols = slice(g * OUTS, (g + 1) * OUTS)
        out_ref[:, cols] = (hid[:, cols] + fb[g]).astype(jnp.bfloat16)
    for copy in sends:
        copy.wait_send()


def on_device(residual, attn_part, norm_gain, routes, gates, gate_weight, up_weight, down_weight):
    bf16, f32 = jnp.bfloat16, jnp.float32
    dma = pltpu.SemaphoreType.DMA
    vmem = pl.BlockSpec(memory_space=pltpu.VMEM)
    hbm = pl.BlockSpec(memory_space=pl.ANY)
    return pl.pallas_call(
        kernel,
        out_shape=jax.ShapeDtypeStruct((TOK, HALF), bf16),
        in_specs=[vmem] * 5 + [hbm] * 3,
        out_specs=vmem,
        scratch_shapes=[
            pltpu.VMEM((D, FFS), bf16),
            pltpu.VMEM((D, FFS), bf16),
            pltpu.VMEM((8 * FFS, OUTS), bf16),
            pltpu.VMEM((2, 16, HALF + QUART), bf16),
            pltpu.VMEM((TOK, HALF), f32),
            pltpu.VMEM((NZ, 16, QUART), bf16),
            pltpu.VMEM((NZ, TOK, 128), f32),
            pltpu.VMEM((NX, TOK, 128), f32),
            pltpu.VMEM((2, NY, 16, HALF), bf16),
            pltpu.VMEM((2, 2, NY, NX, 16, HALF), bf16),
            pltpu.VMEM((256, 2 * FFS), f32),
            pltpu.VMEM((2, 8, 256, FFS), bf16),
            pltpu.VMEM((256, OUTS), f32),
            pltpu.VMEM((2, NY, 4, 16, OUTS), bf16),
            pltpu.VMEM((32, 16, OUTS), bf16),
            pltpu.VMEM((NX, TOK, OUTS), f32),
            pltpu.VMEM((NX, TOK, OUTS), f32),
            dma((3,)),
            dma((1,)),
            dma((1,)),
            dma((NZ,)),
            dma((NZ,)),
            dma((NZ,)),
            dma((NZ,)),
            dma((NX,)),
            dma((NX,)),
            dma((2, NY)),
            dma((2, NY)),
            dma((2, NY, 2)),
            dma((2, NY, 2)),
            dma((2, NY, 2)),
            dma((2, NY, 2)),
            dma((2, NY, 4)),
            dma((2, NY, 4)),
            dma((2, NX)),
            dma((2, NX)),
            dma((2, NX)),
            dma((2, NX)),
            dma((NY, NZ)),
            dma((NY, NZ)),
            dma((NX,)),
            dma((NX,)),
        ],
        compiler_params=pltpu.CompilerParams(
            collective_id=0, has_side_effects=True, vmem_limit_bytes=48 * 2**20
        ),
    )(
        residual,
        attn_part.reshape(TOK, D),
        norm_gain.reshape(1, HALF),
        routes,
        gates,
        gate_weight,
        up_weight,
        down_weight,
    )


def solution(mesh):
    placed = (
        P(("req", "grp"), "head"),
        P("head", ("req", "grp"), None),
        P("head"),
        P(("req", "grp"), None),
        P(("req", "grp"), None),
        P("req", None, ("head", "grp")),
        P("req", None, ("head", "grp")),
        P("req", None, ("head", "grp")),
    )
    return jax.shard_map(
        on_device, mesh=mesh, in_specs=placed, out_specs=P(("req", "grp"), "head"), check_vma=False
    )
```

time: 269 us -> 111 us (0.41)
  waiting for transfers between devices: 165 us -> 0 us
  Pallas kernels: 0 us -> 103 us
  blocking collectives: 56.3 us -> 0 us
  matrix products: 16.5 us -> 0 us
  between operations: 13.2 us -> 0.02 us
  starting transfers between devices: 10.2 us -> 0 us
    all_gather x3 -> x0, waiting for transfers between devices: 123 us -> none  [the longest x1 80 us: on_device(): lax.all_gather(whole_rows[None], 'grp', axis=0, tiled=True)]
    pallas_call x0 -> x1, Pallas kernels: none -> 103 us  [on_device(): pl.pallas_call(kernel, out_shape=jax.ShapeDtypeStruct((TOK, HALF), bf16),...]
    all_to_all x2 -> x0, blocking collectives: 53.8 us -> none  [the longest x1 36 us: on_device(): lax.all_to_all(packed, 'req', split_axis=0, concat_axis=0, tiled=True)]
    all_to_all x1 -> x0, waiting for transfers between devices: 25 us -> none  [on_device(): lax.all_to_all(regrouped, 'req', split_axis=0, concat_axis=0, tiled=True)]
    dot_general x5 -> x0, matrix products: 16.5 us -> none  [the longest x1 6.33 us: expert_hidden(): jnp.einsum('gresd,edf->gresf', shaped, gate_weight, preferred_element_typ...]
    reduce_scatter x1 -> x0, waiting for transfers between devices: 16 us -> none  [on_device(): lax.psum_scatter(attn_part[0].astype(jnp.float32).astype(jnp.bfloat16), '...]
    all_to_all x1 -> x0, starting transfers between devices: 10.1 us -> none  [on_device(): lax.all_to_all(regrouped, 'req', split_axis=0, concat_axis=0, tiled=True)]
    unnamed x10 -> x11, local copies, waits for them, and re-layouts: 0.92 us -> 5.75 us
  transfers between devices with their start and end apart: 5 -> 0, of which waited for: 5 -> 0; matrix products, arithmetic and copies ran while one was open for 1% -> 0% of each run, Pallas kernels for 0% -> 0%
where the time goes in v1:
time: 111 us; the launch traced here: 110 us
  Pallas kernels  103 us (93%)
  local copies, waits for them, and re-layouts  6.48 us (6%)
    pallas_call x1, Pallas kernels, on_device(): pl.pallas_call(kernel, out_shape=jax.ShapeDtypeStruct((TOK, HALF), bf16),...  103 us
    unnamed x11, local copies, waits for them, and re-layouts  5.75 us

profile of v1, /device:TPU:32, one launch (start us, length us, event | category | flops | bytes accessed | tf_op | source)
XLA Modules:
  0.0 109.8 jit_solution(2351779586514105085)
XLA Ops:
  0.0 0.7 reshape.7.gain_ref
  0.7 0.0 copy-start
  0.7 2.0 %copy-done = bf16[1,7168,256]{2,1,0:T(8,128)(2,1)S(1)} copy-done((bf16[1,7168,256]{2,1,0:T(8,128)(2,1)S(1)}, bf16[1,7168,256]{2,1,0:T(8,128)(2,1)}, u32[]{:S(2)}) %copy-start) | copy-done | bytes 3670040
  2.8 0.0 copy-start.1
  2.8 0.9 copy-done.1
  3.7 0.0 copy-start.2
  3.7 0.8 copy-done.2
  4.5 0.0 copy-start.3
  4.5 0.7 copy-done.3
  5.2 0.0 copy-start.4
  5.2 0.7 copy-done.4
  5.9 103.3 %shard_map.82 = bf16[8,3584]{1,0:T(8,128)(2,1)S(1)} custom-call(bf16[8,3584]{1,0:T(8,128)(2,1)S(1)} %copy-done.2, bf16[8,7168]{1,0:T(8,128)(2,1)S(1)} %bitcast.1, f32[1,3584]{1,0:T(1,128)S(1)} %reshape.7.gain_ref, s32[8,8]{1,0:T(8,128)S(1)} %copy-done.3, f32[8,8]{1,0:T(8,128)S(1)} %copy-done.4, bf16[1,7168,256]{2,1,0:T(8,128)(2,1)S(1)} %copy-done, ...), custom_call_target="tpu_custom_call" | custom-call | tf_op jit(solution)/shard_map/pallas_call | solution.py:374
  109.1 0.6 copy.10
Async XLA Ops:
  0.7 2.0 %copy-start = (bf16[1,7168,256]{2,1,0:T(8,128)(2,1)S(1)}, bf16[1,7168,256]{2,1,0:T(8,128)(2,1)}, u32[]{:S(2)}) copy-start(bf16[1,7168,256]{2,1,0:T(8,128)(2,1)} %wg_hbm.1) | copy-start | bytes 11010052
  2.8 0.9 copy-start.1
  3.7 0.8 copy-start.2
  4.5 0.7 copy-start.3
  5.2 0.7 copy-start.4

commit v2 on v1

--- a/solution.py
+++ b/solution.py
@@ -14,35 +14,46 @@
 CAP = 4
 TOK = 8
 NX, NY, NZ = 4, 4, 8
+ROWS = 128
+ZBAR = (1, 2, 4, 6, 7)
+CA = 2560
+CB = HALF - CA
+UA, UB = CA // 2, CB // 2
 FFS = 256
 OUTS = 896
 EPSILON = 1e-06
 
-ZREL = (0, 1, 7, 2, 6, 3, 5, 4)
+ZREL = (0, 2, 6, 4, 1, 7, 3, 5)
 YREL = (0, 1, 3, 2)
 ZSLOT = {rel: slot for slot, rel in enumerate(ZREL)}
 YSLOT = {rel: slot for slot, rel in enumerate(YREL)}
 
 
 def kernel(
+    res_hbm,
+    attn_hbm,
+    gain_hbm,
+    routes_hbm,
+    gates_hbm,
+    wg_hbm,
+    wu_hbm,
+    wd_hbm,
+    out_ref,
     res_ref,
     attn_ref,
     gain_ref,
     routes_ref,
     gates_ref,
-    wg_hbm,
-    wu_hbm,
-    wd_hbm,
-    out_ref,
     wg,
     wu,
     wd,
     ex,
     hid,
+    za,
     zb,
-    zi,
     xi,
     ysel,
+    ybel,
     xb,
     acc,
     hb,
@@ -51,17 +62,22 @@
     rb,
     fs,
     fb,
+    isem,
     wsem,
     ex_s,
     ex_r,
+    za_s,
+    za_r,
     zb_s,
     zb_r,
-    zi_s,
-    zi_r,
+    xb_s,
+    xb_r,
     xi_s,
     xi_r,
     y_s,
     y_r,
+    yb_s,
+    yb_r,
     xn_s,
     xn_r,
     xf_s,
@@ -101,19 +117,29 @@
             src_ref=dst, dst_ref=dst, send_sem=ssem, recv_sem=rsem, device_id=dev(sib=True), device_id_type=MESH
         ).wait_recv()
 
+    pairs = (
+        (attn_hbm.at[0], attn_ref),
+        (res_hbm, res_ref),
+        (routes_hbm, routes_ref),
+        (gates_hbm, gates_ref),
+        (gain_hbm, gain_ref),
+    )
+    inputs = [pltpu.make_async_copy(src, dst, isem.at[i]) for i, (src, dst) in enumerate(pairs)]
+    for copy in inputs:
+        copy.start()
     loads = [
         pltpu.make_async_copy(src.at[0], dst, wsem.at[i])
         for i, (src, dst) in enumerate(((wg_hbm, wg), (wu_hbm, wu), (wd_hbm, wd)))
     ]
-    for load in loads:
-        load.start()
 
     bar = pltpu.get_barrier_semaphore()
     peers = [dev(sib=True)] + [dev(dx=d) for d in range(1, NX)]
-    peers += [dev(dy=a, dz=b) for a in range(NY) for b in range(NZ) if a or b]
+    peers += [dev(dy=d) for d in range(1, NY)] + [dev(dz=d) for d in ZBAR]
     for peer in peers:
         pl.semaphore_signal(bar, inc=1, device_id=peer, device_id_type=MESH)
 
+    for copy in inputs:
+        copy.wait()
     attn = attn_ref[...].astype(jnp.float32)
     res = res_ref[...].astype(jnp.float32)
     ex[0, :, :HALF] = jnp.concatenate([attn[:, :HALF], attn[:, HALF:]], axis=0).astype(jnp.bfloat16)
@@ -133,15 +159,14 @@
     for t in range(TOK - 1):
         before = before + jnp.where(row > t, named[t : t + 1, :], 0.0)
     info = jnp.where(before == (column % CAP).astype(jnp.float32), value, 0.0)
-    zi[0] = info
     xi[x] = info
+    table = jnp.concatenate([info, info], axis=0)
+    table = (table != 0.0).astype(jnp.float32).astype(jnp.bfloat16)
+    za[0, :, UA:] = table
+    zb[0, x, :, UB:] = table
 
     pl.semaphore_wait(bar, len(peers))
     send(ex.at[0], ex.at[1], ex_s.at[0], ex_r.at[0], dev(sib=True))
-    order = [(NZ - ZREL[slot]) % NZ for slot in range(1, NZ)]
-    for d in order:
-        slot = ZSLOT[(-d) % NZ]
-        send(zi.at[0], zi.at[slot], zi_s.at[slot], zi_r.at[slot], dev(dz=d))
     for d in (1, 3, 2):
         send(xi.at[x], xi.at[x], xi_s.at[d], xi_r.at[4 - d], dev(dx=d))
 
@@ -156,54 +181,92 @@
     other = t_res + jnp.where(first, sums[1], sums[0])
     squares = jnp.sum(own * own, axis=1, keepdims=True) + jnp.sum(other * other, axis=1, keepdims=True)
     scale = lax.rsqrt(squares / D + EPSILON)
-    normed = own * scale * gain_ref[...]
+    gain = jnp.concatenate([gain_ref[i : i + 1, :] for i in range(HALF // 128)], axis=1)
+    normed = own * scale * gain
     hid[...] = own
-    zb[0] = jnp.concatenate([normed[:, :QUART], normed[:, QUART:]], axis=0).astype(jnp.bfloat16)
-    for d in order:
+    a_cols, b_cols = normed[:, :CA], normed[:, CA:]
+    za[0, :, :UA] = jnp.concatenate([a_cols[:, :UA], a_cols[:, UA:]], axis=0).astype(jnp.bfloat16)
+    zb[0, x, :, :UB] = jnp.concatenate([b_cols[:, :UB], b_cols[:, UB:]], axis=0).astype(jnp.bfloat16)
+
+    def z_send(buf, ssem, rsem, d):
         slot = ZSLOT[(-d) % NZ]
-        send(zb.at[0], zb.at[slot], zb_s.at[slot], zb_r.at[slot], dev(dz=d))
+        send(buf.at[0], buf.at[slot], ssem.at[slot], rsem.at[slot], dev(dz=d))
+
+    def z_wait(buf, ssem, rsem, rel):
+        slot = ZSLOT[rel]
+        arrived(buf.at[slot], ssem.at[slot], rsem.at[slot])
+
+    def z_relay(buf, ssem, rsem, rel):
+        third, onward = (3, 7) if rel == 2 else (5, 1)
+        slot = ZSLOT[third]
+        send(buf.at[ZSLOT[rel]], buf.at[slot], ssem.at[slot], rsem.at[slot], dev(dz=onward))
+
+    def z_first(buf, ssem, rsem):
+        for rel in (2, 6):
+            z_wait(buf, ssem, rsem, rel)
+            z_relay(buf, ssem, rsem, rel)
+        for d in (7, 1):
+            z_send(buf, ssem, rsem, d)
+        z_wait(buf, ssem, rsem, 4)
+
+    def z_second(buf, ssem, rsem):
+        for rel in (1, 7, 3, 5):
+            z_wait(buf, ssem, rsem, rel)
+
+    for d in (6, 2, 4):
+        z_send(za, za_s, za_r, d)
+    for d in (1, 3, 2):
+        send(zb.at[0, x], zb.at[0, x], xb_s.at[d], xb_r.at[4 - d], dev(dx=d))
 
     left, right = (x + 3) % NX, (x + 1) % NX
 
     def x_send(c, yr):
-        piece = xb.at[c, h, yr, x]
+        piece = xb.at[c, h, yr, x, :, pl.ds(0, CA)]
         send(piece, piece, xn_s.at[c, yr, 0], xn_r.at[c, yr, 0], dev(dx=1))
         send(piece, piece, xn_s.at[c, yr, 1], xn_r.at[c, yr, 1], dev(dx=3))
         send(piece, piece, sib_s.at[c, yr, 0], sib_r.at[c, yr, 0], dev(sib=True))
 
     def x_forward(c, yr):
         for way, source, to in ((0, left, 1), (1, right, 3)):
-            piece = xb.at[c, h, yr, source]
+            piece = xb.at[c, h, yr, source, :, pl.ds(0, CA)]
             arrived(piece, xn_s.at[c, yr, way], xn_r.at[c, yr, way])
-            part = xb.at[c, h, yr, source, :, pl.ds(way * QUART, QUART)]
+            part = xb.at[c, h, yr, source, :, pl.ds(way * UA, UA)]
             send(part, part, xf_s.at[c, yr, way], xf_r.at[c, yr, way], dev(dx=to))
             send(piece, piece, sib_s.at[c, yr, 1 + way], sib_r.at[c, yr, 1 + way], dev(sib=True))
 
     def x_far(c, yr):
         far = (x + 2) % NX
         for way in (0, 1):
-            part = xb.at[c, h, yr, far, :, pl.ds(way * QUART, QUART)]
+            part = xb.at[c, h, yr, far, :, pl.ds(way * UA, UA)]
             arrived(part, xf_s.at[c, yr, way], xf_r.at[c, yr, way])
-        piece = xb.at[c, h, yr, far]
+        piece = xb.at[c, h, yr, far, :, pl.ds(0, CA)]
         send(piece, piece, sib_s.at[c, yr, 3], sib_r.at[c, yr, 3], dev(sib=True))
 
-    def sib_wait(c):
-        for yr in range(NY):
+    def sib_wait(k):
+        c = k // 2
+        for yr in (k % 2 * 2, k % 2 * 2 + 1):
             for kind, source in enumerate((x, left, right, (x + 2) % NX)):
-                piece = xb.at[c, 1 - h, yr, source]
+                piece = xb.at[c, 1 - h, yr, source, :, pl.ds(0, CA)]
                 arrived(piece, sib_s.at[c, yr, kind], sib_r.at[c, yr, kind])
+            arrived(b_rows(c, 1 - h, yr), sib_s.at[c, yr, 4], sib_r.at[c, yr, 4])
 
     def y_wait(c, yr):
-        piece = xb.at[c, h, yr, x]
+        piece = xb.at[c, h, yr, x, :, pl.ds(0, CA)]
         arrived(piece, y_s.at[c, yr], y_r.at[c, yr])
 
-    def select(c):
-        for slot in range(4 * c, 4 * c + 4):
-            if slot:
-                arrived(zi.at[slot], zi_s.at[slot], zi_r.at[slot])
-                arrived(zb.at[slot], zb_s.at[slot], zb_r.at[slot])
-        tables = [(zi[4 * c + j] != 0.0).astype(jnp.bfloat16) for j in range(4)]
-        table = jnp.concatenate([t for j in range(4) for t in (tables[j], tables[j])], axis=0)
+    def b_rows(c, half_index, yr):
+        return xb.at[c, half_index, yr, :, :, pl.ds(CA, CB)]
+
+    def b_sib(c, yr):
+        piece = b_rows(c, h, yr)
+        send(piece, piece, sib_s.at[c, yr, 4], sib_r.at[c, yr, 4], dev(sib=True))
+
+    def b_wait(c, yr):
+        arrived(b_rows(c, h, yr), yb_s.at[c, yr], yb_r.at[c, yr])
+        b_sib(c, yr)
+
+    def choose(tables, blocks):
+        table = jnp.concatenate(tables, axis=0)
         rows16 = lax.broadcasted_iota(jnp.int32, (16, 128), 0) % CAP
         cols16 = lax.broadcasted_iota(jnp.int32, (16, 128), 1)
         pick = jnp.concatenate(
@@ -218,26 +281,52 @@
         )
         r = lax.broadcasted_iota(jnp.int32, (64, 64), 0)
         m = lax.broadcasted_iota(jnp.int32, (64, 64), 1)
-        blocks = zb[4 * c : 4 * c + 4].reshape(64, QUART)
+        chosen = []
         for u in (0, 1):
             mask = ((r // 4) % 4 == m // 16) & ((m // 8) % 2 == u)
             onehot = jnp.where(mask, small, 0.0).astype(jnp.bfloat16)
-            rows = jnp.dot(onehot, blocks, preferred_element_type=jnp.float32).astype(jnp.bfloat16)
-            cols = slice(u * QUART, (u + 1) * QUART)
-            xb[c, h, 0, x, :, cols] = rows[:16]
+            chosen.append(jnp.dot(onehot, blocks, preferred_element_type=jnp.float32).astype(jnp.bfloat16))
+        return chosen
+
+    def select_a(c):
+        group = range(4 * c, 4 * c + 4)
+        chosen = choose([za[slot, :, UA:] for slot in group], za[4 * c : 4 * c + 4, :, :UA].reshape(64, UA))
+        for u in (0, 1):
+            xb[c, h, 0, x, :, u * UA : (u + 1) * UA] = chosen[u][:16]
             for yr in range(1, NY):
-                ysel[c, yr, :, cols] = rows[16 * yr : 16 * yr + 16]
+                ysel[c, yr, :, u * UA : (u + 1) * UA] = chosen[u][16 * yr : 16 * yr + 16]
         for yr in (1, 2, 3):
             back = YSLOT[(-YREL[yr]) % NY]
-            send(ysel.at[c, yr], xb.at[c, h, back, x], y_s.at[c, back], y_r.at[c, back], dev(dy=YREL[yr]))
-        x_send(c, 0)
-
-    def up(c):
+            send(
+                ysel.at[c, yr],
+                xb.at[c, h, back, x, :, pl.ds(0, CA)],
+                y_s.at[c, back],
+                y_r.at[c, back],
+                dev(dy=YREL[yr]),
+            )
+
+    def select_b(c):
+        group = range(4 * c, 4 * c + 4)
+        for xs in range(NX):
+            chosen = choose(
+                [zb[slot, xs, :, UB:] for slot in group], zb[4 * c : 4 * c + 4, xs, :, :UB].reshape(64, UB)
+            )
+            for u in (0, 1):
+                xb[c, h, 0, xs, :, CA + u * UB : CA + (u + 1) * UB] = chosen[u][:16]
+                for yr in range(1, NY):
+                    ybel[c, yr, xs, :, u * UB : (u + 1) * UB] = chosen[u][16 * yr : 16 * yr + 16]
+        for yr in (1, 2, 3):
+            back = YSLOT[(-YREL[yr]) % NY]
+            send(ybel.at[c, yr], b_rows(c, h, back), yb_s.at[c, back], yb_r.at[c, back], dev(dy=YREL[yr]))
+        b_sib(c, 0)
+
+    def up(k):
+        c, yp = k // 2, k % 2 * 2
         acc[...] = jnp.zeros_like(acc)
 
         def step(i, carry):
-            part = xb[c, i // 2, :, :, :, pl.ds(pl.multiple_of((i % 2) * QUART, QUART), QUART)]
-            rows = part.reshape(256, QUART)
+            part = xb[c, i // 2, yp : yp + 2, :, :, pl.ds(pl.multiple_of((i % 2) * QUART, QUART), QUART)]
+            rows = part.reshape(ROWS, QUART)
             ks = pl.ds(pl.multiple_of(i * QUART, QUART), QUART)
             acc[:, :FFS] += jnp.dot(rows, wg[ks, :], preferred_element_type=jnp.float32)
             acc[:, FFS:] += jnp.dot(rows, wu[ks, :], preferred_element_type=jnp.float32)
@@ -245,41 +334,42 @@
 
         lax.fori_loop(0, 4, step, 0)
         gate = acc[:, :FFS]
-        hb[c, h * NX + x] = (gate / (1.0 + jnp.exp(-gate)) * acc[:, FFS:]).astype(jnp.bfloat16)
-        mine = hb.at[c, h * NX + x]
+        hb[k, h * NX + x] = (gate / (1.0 + jnp.exp(-gate)) * acc[:, FFS:]).astype(jnp.bfloat16)
+        mine = hb.at[k, h * NX + x]
         for d in (1, 3, 2):
-            send(mine, mine, h_s.at[c, d], h_r.at[c, 4 - d], dev(dx=d))
-        send(mine, mine, hs_s.at[c, 0], hs_r.at[c, 0], dev(sib=True))
-
-    def h_forward(c):
+            send(mine, mine, h_s.at[k, d], h_r.at[k, 4 - d], dev(dx=d))
+        send(mine, mine, hs_s.at[k, 0], hs_r.at[k, 0], dev(sib=True))
+
+    def h_forward(k):
         for d in (1, 3, 2):
-            block = hb.at[c, h * NX + (x + d) % NX]
-            arrived(block, h_s.at[c, d], h_r.at[c, d])
-            send(block, block, hs_s.at[c, d], hs_r.at[c, d], dev(sib=True))
-
-    def down(c):
+            block = hb.at[k, h * NX + (x + d) % NX]
+            arrived(block, h_s.at[k, d], h_r.at[k, d])
+            send(block, block, hs_s.at[k, d], hs_r.at[k, d], dev(sib=True))
+
+    def down(k):
+        c, yp = k // 2, k % 2 * 2
         for d in (0, 1, 3, 2):
-            block = hb.at[c, (1 - h) * NX + (x + d) % NX]
-            arrived(block, hs_s.at[c, d], hs_r.at[c, d])
+            block = hb.at[k, (1 - h) * NX + (x + d) % NX]
+            arrived(block, hs_s.at[k, d], hs_r.at[k, d])
         for start, width in ((0, 512), (512, 384)):
-            total = jnp.zeros((256, width), jnp.float32)
+            total = jnp.zeros((ROWS, width), jnp.float32)
             for b in range(8):
                 total = total + jnp.dot(
-                    hb[c, b],
+                    hb[k, b],
                     wd[b * FFS : (b + 1) * FFS, start : start + width],
                     preferred_element_type=jnp.float32,
                 )
             dacc[:, start : start + width] = total
-        for yr in range(NY):
+        for yi in range(2):
             for j in range(4):
+                yr, slot = yp + yi, 4 * c + j
                 rows = jnp.concatenate(
                     [
-                        dacc[yr * 64 + xs * 16 + j * 4 : yr * 64 + xs * 16 + j * 4 + 4, :]
+                        dacc[yi * 64 + xs * 16 + j * 4 : yi * 64 + xs * 16 + j * 4 + 4, :]
                         for xs in range(NX)
                     ],
                     axis=0,
                 ).astype(jnp.bfloat16)
-                slot = 4 * c + j
                 if yr == 0 and slot == 0:
                     rb[req] = rows
                 else:
@@ -292,40 +382,64 @@
                         dev(dy=YREL[yr], dz=ZREL[slot]),
                     )
 
-    select(0)
-    y_wait(0, 1)
-    x_send(0, 1)
-    y_wait(0, 2)
-    x_send(0, 2)
-    y_wait(0, 3)
-    x_send(0, 3)
+    for d in (1, 3, 2):
+        arrived(zb.at[0, (x + d) % NX], xb_s.at[d], xb_r.at[d])
+    for d in (6, 2, 4):
+        z_send(zb, zb_s, zb_r, d)
+    for load in loads:
+        load.start()
+    z_first(za, za_s, za_r)
+    select_a(0)
+    x_send(0, 0)
+    for yr in (1, 2, 3):
+        y_wait(0, yr)
+        x_send(0, yr)
+    z_first(zb, zb_s, zb_r)
     x_forward(0, 0)
-    select(1)
+    select_b(0)
+    z_second(za, za_s, za_r)
+    select_a(1)
+    x_send(1, 0)
     x_forward(0, 1)
-    y_wait(1, 1)
-    x_send(1, 1)
-    y_wait(1, 2)
-    x_send(1, 2)
     x_forward(0, 2)
-    y_wait(1, 3)
-    x_send(1, 3)
     x_forward(0, 3)
-    for yr in range(NY):
-        x_far(0, yr)
+    for yr in (1, 2, 3):
+        y_wait(1, yr)
+        x_send(1, yr)
+    b_wait(0, 1)
+    b_wait(0, 2)
+    b_wait(0, 3)
+    z_second(zb, zb_s, zb_r)
+    select_b(1)
     for load in loads:
         load.wait()
-    x_forward(1, 0)
+    x_far(0, 0)
+    x_far(0, 1)
     sib_wait(0)
     up(0)
+    x_far(0, 2)
+    x_far(0, 3)
+    sib_wait(1)
+    up(1)
+    x_forward(1, 0)
     x_forward(1, 1)
     x_forward(1, 2)
-    x_forward(1, 3)
     h_forward(0)
     down(0)
-    for yr in range(NY):
-        x_far(1, yr)
-    sib_wait(1)
-    up(1)
+    x_forward(1, 3)
+    h_forward(1)
+    down(1)
+    b_wait(1, 1)
+    b_wait(1, 2)
+    b_wait(1, 3)
+    x_far(1, 0)
+    x_far(1, 1)
+    sib_wait(2)
+    up(2)
+    x_far(1, 2)
+    x_far(1, 3)
+    sib_wait(3)
+    up(3)
 
     for d in (1, 3, 2):
         arrived(xi.at[(x + d) % NX], xi_s.at[d], xi_r.at[d])
@@ -343,8 +457,10 @@
         for part in (high, low)
     ]
 
-    h_forward(1)
-    down(1)
+    h_forward(2)
+    down(2)
+    h_forward(3)
+    down(3)
     for yr in range(NY):
         for slot in range(NZ):
             if yr or slot:
@@ -374,26 +490,33 @@
     return pl.pallas_call(
         kernel,
         out_shape=jax.ShapeDtypeStruct((TOK, HALF), bf16),
-        in_specs=[vmem] * 5 + [hbm] * 3,
+        in_specs=[hbm] * 8,
         out_specs=vmem,
         scratch_shapes=[
+            pltpu.VMEM((TOK, HALF), bf16),
+            pltpu.VMEM((TOK, D), bf16),
+            pltpu.VMEM((HALF // 128, 128), f32),
+            pltpu.VMEM((TOK, TOK), jnp.int32),
+            pltpu.VMEM((TOK, TOK), f32),
             pltpu.VMEM((D, FFS), bf16),
             pltpu.VMEM((D, FFS), bf16),
             pltpu.VMEM((8 * FFS, OUTS), bf16),
             pltpu.VMEM((2, 16, HALF + QUART), bf16),
             pltpu.VMEM((TOK, HALF), f32),
-            pltpu.VMEM((NZ, 16, QUART), bf16),
-            pltpu.VMEM((NZ, TOK, 128), f32),
+            pltpu.VMEM((NZ, 16, UA + 128), bf16),
+            pltpu.VMEM((NZ, NX, 16, UB + 128), bf16),
             pltpu.VMEM((NX, TOK, 128), f32),
-            pltpu.VMEM((2, NY, 16, HALF), bf16),
+            pltpu.VMEM((2, NY, 16, CA), bf16),
+            pltpu.VMEM((2, NY, NX, 16, CB), bf16),
             pltpu.VMEM((2, 2, NY, NX, 16, HALF), bf16),
-            pltpu.VMEM((256, 2 * FFS), f32),
-            pltpu.VMEM((2, 8, 256, FFS), bf16),
-            pltpu.VMEM((256, OUTS), f32),
+            pltpu.VMEM((ROWS, 2 * FFS), f32),
+            pltpu.VMEM((4, 8, ROWS, FFS), bf16),
+            pltpu.VMEM((ROWS, OUTS), f32),
             pltpu.VMEM((2, NY, 4, 16, OUTS), bf16),
             pltpu.VMEM((32, 16, OUTS), bf16),
             pltpu.VMEM((NX, TOK, OUTS), f32),
             pltpu.VMEM((NX, TOK, OUTS), f32),
+            dma((5,)),
             dma((3,)),
             dma((1,)),
             dma((1,)),
@@ -403,30 +526,34 @@
             dma((NZ,)),
             dma((NX,)),
             dma((NX,)),
+            dma((NX,)),
+            dma((NX,)),
+            dma((2, NY)),
+            dma((2, NY)),
             dma((2, NY)),
             dma((2, NY)),
             dma((2, NY, 2)),
             dma((2, NY, 2)),
             dma((2, NY, 2)),
             dma((2, NY, 2)),
-            dma((2, NY, 4)),
-            dma((2, NY, 4)),
-            dma((2, NX)),
-            dma((2, NX)),
-            dma((2, NX)),
-            dma((2, NX)),
+            dma((2, NY, 5)),
+            dma((2, NY, 5)),
+            dma((4, NX)),
+            dma((4, NX)),
+            dma((4, NX)),
+            dma((4, NX)),
             dma((NY, NZ)),
             dma((NY, NZ)),
             dma((NX,)),
             dma((NX,)),
         ],
         compiler_params=pltpu.CompilerParams(
-            collective_id=0, has_side_effects=True, vmem_limit_bytes=48 * 2**20
+            collective_id=0, has_side_effects=True, vmem_limit_bytes=60 * 2**20
         ),
     )(
         residual,
-        attn_part.reshape(TOK, D),
-        norm_gain.reshape(1, HALF),
+        attn_part,
+        norm_gain.reshape(HALF // 128, 128),
         routes,
         gates,
         gate_weight,

time: 111 us -> 86.4 us (0.78)
  the two profiles are of different devices: /device:TPU:32 before, /device:TPU:1 now
where the time goes in v2:
time: 86.4 us; the launch traced here: 86.3 us
  Pallas kernels  84.8 us (98%)
  local copies, waits for them, and re-layouts  1.45 us (2%)
    pallas_call x1, Pallas kernels, on_device(): pl.pallas_call(kernel, out_shape=jax.ShapeDtypeStruct((TOK, HALF), bf16),...  84.8 us

profile of v2, /device:TPU:1, one launch (start us, length us, event | category | flops | bytes accessed | tf_op | source)
XLA Modules:
  0.0 86.3 jit_solution(4878776532495487519)
XLA Ops:
  0.0 84.8 %shard_map.82 = bf16[8,3584]{1,0:T(8,128)(2,1)} custom-call(bf16[8,3584]{1,0:T(8,128)(2,1)} %res_hbm.1, bf16[1,8,7168]{2,1,0:T(8,128)(2,1)} %attn_hbm.1, f32[28,128]{1,0:T(8,128)} %bitcast.1, s32[8,8]{1,0:T(8,128)} %routes_hbm.1, f32[8,8]{1,0:T(8,128)} %gates_hbm.1, bf16[1,7168,256]{2,1,0:T(8,128)(2,1)} %wg_hbm.1, bf16[1,7168,256]{2,1,0:T(8,128)(2,1)} %wu_hbm.1, ...), custom_call_target="tpu_custom_call" | custom-call | tf_op jit(solution)/shard_map/pallas_call | solution.py:490
  84.8 1.4 %copy.10 = bf16[8,3584]{1,0:T(8,128)(2,1)} copy(bf16[8,3584]{1,0:T(8,128)(2,1)} %shard_map.82) | data formatting | bytes 114688

commit v3 on v2

--- a/solution.py
+++ b/solution.py
@@ -15,7 +15,7 @@
 TOK = 8
 NX, NY, NZ = 4, 4, 8
 ROWS = 128
-ZBAR = (1, 2, 4, 6, 7)
+ZBAR = (1, 2, 3, 4, 5, 6, 7)
 CA = 2560
 CB = HALF - CA
 UA, UB = CA // 2, CB // 2
@@ -23,7 +23,7 @@
 OUTS = 896
 EPSILON = 1e-06
 
-ZREL = (0, 2, 6, 4, 1, 7, 3, 5)
+ZREL = (0, 4, 3, 5, 1, 7, 2, 6)
 YREL = (0, 1, 3, 2)
 ZSLOT = {rel: slot for slot, rel in enumerate(ZREL)}
 YSLOT = {rel: slot for slot, rel in enumerate(YREL)}
@@ -196,24 +196,17 @@
         slot = ZSLOT[rel]
         arrived(buf.at[slot], ssem.at[slot], rsem.at[slot])
 
-    def z_relay(buf, ssem, rsem, rel):
-        third, onward = (3, 7) if rel == 2 else (5, 1)
-        slot = ZSLOT[third]
-        send(buf.at[ZSLOT[rel]], buf.at[slot], ssem.at[slot], rsem.at[slot], dev(dz=onward))
-
     def z_first(buf, ssem, rsem):
-        for rel in (2, 6):
+        for rel in (3, 5, 4):
             z_wait(buf, ssem, rsem, rel)
-            z_relay(buf, ssem, rsem, rel)
-        for d in (7, 1):
+        for d in (7, 1, 6, 2):
             z_send(buf, ssem, rsem, d)
-        z_wait(buf, ssem, rsem, 4)
 
     def z_second(buf, ssem, rsem):
-        for rel in (1, 7, 3, 5):
+        for rel in (1, 7, 2, 6):
             z_wait(buf, ssem, rsem, rel)
 
-    for d in (6, 2, 4):
+    for d in (5, 3, 4):
         z_send(za, za_s, za_r, d)
     for d in (1, 3, 2):
         send(zb.at[0, x], zb.at[0, x], xb_s.at[d], xb_r.at[4 - d], dev(dx=d))
@@ -384,7 +377,7 @@
 
     for d in (1, 3, 2):
         arrived(zb.at[0, (x + d) % NX], xb_s.at[d], xb_r.at[d])
-    for d in (6, 2, 4):
+    for d in (5, 3, 4):
         z_send(zb, zb_s, zb_r, d)
     for load in loads:
         load.start()
@@ -452,10 +445,13 @@
     tr = lax.broadcasted_iota(jnp.int32, (32, 512), 0)
     tc = lax.broadcasted_iota(jnp.int32, (32, 512), 1)
     keep = tr // TOK == (tc // CAP) % NX
-    wide = [
-        jnp.where(keep, jnp.dot(part, spread, preferred_element_type=jnp.float32), 0.0).astype(jnp.bfloat16)
-        for part in (high, low)
-    ]
+    wide = jnp.concatenate(
+        [
+            jnp.where(keep, jnp.dot(part, spread, preferred_element_type=jnp.float32), 0.0)
+            for part in (high, low)
+        ],
+        axis=0,
+    ).astype(jnp.bfloat16)
 
     h_forward(2)
     down(2)
@@ -467,9 +463,8 @@
                 source = ((y - YREL[yr]) % NY) * NZ + (z - ZREL[slot]) % NZ
                 arrived(rb.at[source], r_s.at[yr, slot], r_r.at[yr, slot])
     back = rb[...].reshape(512, OUTS)
-    mixed = jnp.dot(wide[0], back, preferred_element_type=jnp.float32)
-    mixed = mixed + jnp.dot(wide[1], back, preferred_element_type=jnp.float32)
-    fs[...] = mixed.reshape(NX, TOK, OUTS)
+    mixed = jnp.dot(wide, back, preferred_element_type=jnp.float32)
+    fs[...] = (mixed[: NX * TOK] + mixed[NX * TOK :]).reshape(NX, TOK, OUTS)
     fb[x] = fs[x]
     for d in (1, 3, 2):
         send(fs.at[(x + d) % NX], fb.at[x], f_s.at[d], f_r.at[4 - d], dev(dx=d))

time: 86.4 us -> 85.5 us (0.990)
  the two profiles are of different devices: /device:TPU:1 before, /device:TPU:32 now
where the time goes in v3:
time: 85.5 us; the launch traced here: 84.9 us
  Pallas kernels  83.4 us (98%)
  local copies, waits for them, and re-layouts  1.45 us (2%)
    pallas_call x1, Pallas kernels, on_device(): pl.pallas_call(kernel, out_shape=jax.ShapeDtypeStruct((TOK, HALF), bf16),...  83.4 us

profile of v3, /device:TPU:32, one launch (start us, length us, event | category | flops | bytes accessed | tf_op | source)
XLA Modules:
  0.0 84.9 jit_solution(7808360014909969988)
XLA Ops:
  0.0 83.4 %shard_map.82 = bf16[8,3584]{1,0:T(8,128)(2,1)} custom-call(bf16[8,3584]{1,0:T(8,128)(2,1)} %res_hbm.1, bf16[1,8,7168]{2,1,0:T(8,128)(2,1)} %attn_hbm.1, f32[28,128]{1,0:T(8,128)} %bitcast.1, s32[8,8]{1,0:T(8,128)} %routes_hbm.1, f32[8,8]{1,0:T(8,128)} %gates_hbm.1, bf16[1,7168,256]{2,1,0:T(8,128)(2,1)} %wg_hbm.1, bf16[1,7168,256]{2,1,0:T(8,128)(2,1)} %wu_hbm.1, ...), custom_call_target="tpu_custom_call" | custom-call | tf_op jit(solution)/shard_map/pallas_call | solution.py:485
  83.4 1.4 %copy.10 = bf16[8,3584]{1,0:T(8,128)(2,1)} copy(bf16[8,3584]{1,0:T(8,128)(2,1)} %shard_map.82) | data formatting | bytes 114688
